TPU v7x, 32 devices: a whole 2x2x4 slice. The times are simulated.
32 devices in a mesh: out: 4 (over y, x), inp: 8 (over z, core).
Axes of the slice: x: 2, y: 2, z: 4, core: 2. Of those that a mesh axis runs over, the one named last changes fastest.
Arguments:
- grads: bfloat16 [512, 28672], P('out', 'inp'), may hold values from -1.1953125 to 1.1953125
- acts: bfloat16 [512, 8192], P('inp', 'out'), may hold values from -6 to 6
- basis_out: bfloat16 [28672, 14336], P('inp', 'out'), may hold values from -0.03125 to 0.03125
- basis_in: bfloat16 [8192, 8192], P('out', 'inp'), may hold values from -0.0625 to 0.0625
- old_correction: float32 [14336, 8192], P('out', 'inp'), may hold values from 0.1 to 2
- lengths: int32 [4], replicated, may hold values from 1 to 256, 512 in all
Outputs:
- correction: float32 [14336, 8192], P('out', 'inp')
Inputs may be any that keep to these rules, and one draw needn't show every extreme that they name: The lengths sum to 512; the longest example has exactly 256 tokens.
All inputs are finite; a program needn't handle non-finite values.
Results may differ from a plain program's by a relative error of at most 0.0021.
Values may be sent and summed in bfloat16 or wider, within the bound.
A program may use at most 128 MiB of HBM per device.

v0:
```python
import jax
import jax.numpy as jnp
from jax import lax
from jax.sharding import PartitionSpec as P

CAP = 256


def body(grads, acts, basis_out, basis_in, old_correction, lengths):
    gathered = lax.all_gather(grads, "out", axis=0, tiled=True)
    row_count = gathered.shape[0]
    scattered = lax.psum_scatter(
        lax.dot_general(
            basis_out, gathered, (((0,), (1,)), ((), ())), preferred_element_type=jnp.float32
        ),
        "inp",
        scatter_dimension=0,
        tiled=True,
    )
    grad_rot = lax.all_gather(scattered.astype(jnp.bfloat16), "inp", axis=0, tiled=True)
    token_dim = 1
    gathered_acts = lax.all_gather(acts, "inp", axis=0, tiled=True)
    act_scattered = lax.psum_scatter(
        jnp.dot(gathered_acts, basis_in, preferred_element_type=jnp.float32),
        "out",
        scatter_dimension=0,
        tiled=True,
    )
    act_rot = lax.all_gather(act_scattered.astype(jnp.bfloat16), "out", axis=0, tiled=True)
    offsets = jnp.cumsum(lengths) - lengths
    examples = lengths.shape[0]

    def add_example(example, running):
        offset = offsets[example]
        length = lengths[example]
        first_row = jnp.minimum(offset, row_count - CAP)
        places = first_row + jnp.arange(CAP, dtype=jnp.int32)
        inside = (places >= offset) & (places < offset + length)
        grad_block = lax.dynamic_slice_in_dim(grad_rot, first_row, CAP, token_dim)
        act_block = lax.dynamic_slice_in_dim(act_rot, first_row, CAP, 0)
        act_block = jnp.where(inside[:, None], act_block, jnp.zeros((), act_block.dtype))
        projected = lax.dot_general(
            grad_block,
            act_block,
            (((token_dim,), (0,)), ((), ())),
            preferred_element_type=jnp.float32,
        )
        return running + projected * projected

    running = lax.fori_loop(0, examples, add_example, jnp.zeros(old_correction.shape, jnp.float32))
    return 0.8 * old_correction + 0.2 * running / examples


def solution(mesh):
    in_specs = (
        P("out", "inp"),
        P("inp", "out"),
        P("inp", "out"),
        P("out", "inp"),
        P("out", "inp"),
        P(),
    )
    out_specs = P("out", "inp")
    return jax.shard_map(body, mesh=mesh, in_specs=in_specs, out_specs=out_specs, check_vma=False)
```

profile of v0, /device:TPU:0, one launch (start us, length us, event | category | flops | bytes accessed | tf_op | source)
XLA Modules:
  0.0 369.8 jit_solution(1507827030369205152)
XLA Ops:
  6.5 0.0 all-gather.9.cloned.1.call-start
  6.5 0.7 all-gather.9.cloned.1.call-update
  7.3 0.0 all-gather.5.cloned.1.call-start
  7.3 0.7 all-gather.5.cloned.1.call-update
  8.0 0.0 reduce-scatter.5.cloned.1.call-start
  8.1 32.7 %all-gather.9.cloned.1.call-done = bf16[512,2048]{1,0:T(8,128)(2,1)} async-done(((bf16[64,2048]{1,0:T(8,128)(2,1)}), bf16[512,2048]{1,0:T(8,128)(2,1)}) %all-gather.9.cloned.1.call-update) | async-done | bytes 2097168 | tf_op jit(solution)/shard_map/all_gather | solution.py:22
  40.8 6.5 %fusion.8 = f32[512,1024]{1,0:T(8,128)} fusion(bf16[512,2048]{1,0:T(8,128)(2,1)} %all-gather.9.cloned.1.call-done, bf16[2048,1024]{1,0:T(8,128)(2,1)} %param.11), kind=kOutput, calls=%fused_computation.12 | convolution fusion | flops 2147483648 | bytes 8388608 | tf_op jit(solution)/shard_map/dot_general | solution.py:24
  47.3 0.0 reduce-scatter.5.cloned.1.call-update
  47.3 0.0 copy-start
  47.3 0.0 reduce-scatter.3.cloned.1.call-start
  47.4 43.1 %all-gather.5.cloned.1.call-done = bf16[512,3584]{1,0:T(8,128)(2,1)} async-done(((bf16[128,3584]{1,0:T(8,128)(2,1)}), bf16[512,3584]{1,0:T(8,128)(2,1)}) %all-gather.5.cloned.1.call-update) | async-done | bytes 3670032 | tf_op jit(solution)/shard_map/all_gather | solution.py:10
  90.5 21.5 %fusion.7 = f32[3584,512]{1,0:T(8,128)} fusion(bf16[3584,3584]{1,0:T(8,128)(2,1)} %param.10, bf16[512,3584]{1,0:T(8,128)(2,1)} %all-gather.5.cloned.1.call-done), kind=kOutput, calls=%fused_computation.11 | convolution fusion | flops 13153337344 | bytes 36700160 | tf_op jit(solution)/shard_map/dot_general | solution.py:13
  112.0 0.0 reduce-scatter.3.cloned.1.call-update
  112.1 0.0 all-gather.11.cloned.1.call-start
  112.1 16.6 %reduce-scatter.5.cloned.1.call-done = f32[128,1024]{1,0:T(8,128)} async-done(((f32[512,1024]{1,0:T(8,128)}), f32[128,1024]{1,0:T(8,128)}) %reduce-scatter.5.cloned.1.call-update) | async-done | bytes 524304 | tf_op jit(solution)/shard_map/reduce_scatter | solution.py:23
  128.7 1.8 convert_element_type.7
  130.5 0.0 all-gather.11.cloned.1.call-update
  130.5 0.2 all-gather.7.cloned.1.call-start
  130.7 80.0 %reduce-scatter.3.cloned.1.call-done = f32[448,512]{1,0:T(8,128)} async-done(((f32[3584,512]{1,0:T(8,128)}), f32[448,512]{1,0:T(8,128)}) %reduce-scatter.3.cloned.1.call-update) | async-done | bytes 917520 | tf_op jit(solution)/shard_map/reduce_scatter | solution.py:12
  210.7 2.0 convert_element_type.6
  212.7 0.0 all-gather.7.cloned.1.call-update
  212.7 0.0 copy-done
  212.8 0.2 reduce-window.9
  212.9 24.6 %all-gather.11.cloned.1.call-done = bf16[512,1024]{1,0:T(8,128)(2,1)} async-done(((bf16[128,1024]{1,0:T(8,128)(2,1)}), bf16[512,1024]{1,0:T(8,128)(2,1)}) %all-gather.11.cloned.1.call-update) | async-done | bytes 1048592 | tf_op jit(solution)/shard_map/all_gather | solution.py:29
  237.6 44.2 %all-gather.7.cloned.1.call-done = bf16[3584,512]{1,0:T(8,128)(2,1)} async-done(((bf16[448,512]{1,0:T(8,128)(2,1)}), bf16[3584,512]{1,0:T(8,128)(2,1)}) %all-gather.7.cloned.1.call-update) | async-done | bytes 3670032 | tf_op jit(solution)/shard_map/all_gather | solution.py:20
  281.8 65.7 %while.14 = (s32[]{:T(128)}, f32[3584,1024]{1,0:T(8,128)}, s32[4]{0:T(128)S(1)}, bf16[3584,512]{1,0:T(8,128)(2,1)}, s32[4]{0:T(128)S(1)}, /*index=5*/bf16[512,10...) while((s32[]{:T(128)}, f32[3584,1024]{1,0:T(8,128)}, s32[4]{0:T(128)S(1)}, ...), condition=%wide.region_4.5_spmd.clone, body=%wide.region_3.4_spmd.clone.sunk | while | flops 1890321408 | bytes 31721684 | solution.py:50
  281.8 0.5 dynamic_slice.44
  282.9 0.7 dynamic_slice.45
  284.8 0.5 compare_and_fusion.2
  285.3 9.8 %select_add_fusion.2 = f32[3584,1024]{1,0:T(8,128)} fusion(f32[3584,1024]{1,0:T(8,128)} %get-tuple-element.196, pred[]{:T(512)S(6)} %compare.3, bf16[3584,512]{1,0:T(8,128)(2,1)} %get-tuple-element.208, s32[]{:T(128)S(6)} %select_n.29, bf16[512,1024]{1,0:T(8,128)(2,1)} %get-tuple-element.210, pred[256]{0:T(512)(128)(4,1)S(1)} %compare_and_fusion.2), kind=kOutput, calls=%fused_computation.clone.1 | convolution fusion | flops 1890320384 | bytes 31721216 | tf_op jit(solution)/shard_map/while/body/eval_jaxpr/dot_general | solution.py:42
  295.1 0.5 dynamic_slice.44
  296.2 0.7 dynamic_slice.45
  298.1 0.5 compare_and_fusion.2
  298.7 14.1 %select_add_fusion.2 = f32[3584,1024]{1,0:T(8,128)} fusion(f32[3584,1024]{1,0:T(8,128)} %get-tuple-element.196, pred[]{:T(512)S(6)} %compare.3, bf16[3584,512]{1,0:T(8,128)(2,1)} %get-tuple-element.208, s32[]{:T(128)S(6)} %select_n.29, bf16[512,1024]{1,0:T(8,128)(2,1)} %get-tuple-element.210, pred[256]{0:T(512)(128)(4,1)S(1)} %compare_and_fusion.2), kind=kOutput, calls=%fused_computation.clone.1 | convolution fusion | flops 1890320384 | bytes 31721216 | tf_op jit(solution)/shard_map/while/body/eval_jaxpr/dot_general | solution.py:42
  312.7 0.5 dynamic_slice.44
  313.9 0.7 dynamic_slice.45
  315.8 0.5 compare_and_fusion.2
  316.3 13.8 %select_add_fusion.2 = f32[3584,1024]{1,0:T(8,128)} fusion(f32[3584,1024]{1,0:T(8,128)} %get-tuple-element.196, pred[]{:T(512)S(6)} %compare.3, bf16[3584,512]{1,0:T(8,128)(2,1)} %get-tuple-element.208, s32[]{:T(128)S(6)} %select_n.29, bf16[512,1024]{1,0:T(8,128)(2,1)} %get-tuple-element.210, pred[256]{0:T(512)(128)(4,1)S(1)} %compare_and_fusion.2), kind=kOutput, calls=%fused_computation.clone.1 | convolution fusion | flops 1890320384 | bytes 31721216 | tf_op jit(solution)/shard_map/while/body/eval_jaxpr/dot_general | solution.py:42
  330.1 0.5 dynamic_slice.44
  331.2 0.7 dynamic_slice.45
  333.1 0.5 compare_and_fusion.2
  333.7 13.8 %select_add_fusion.2 = f32[3584,1024]{1,0:T(8,128)} fusion(f32[3584,1024]{1,0:T(8,128)} %get-tuple-element.196, pred[]{:T(512)S(6)} %compare.3, bf16[3584,512]{1,0:T(8,128)(2,1)} %get-tuple-element.208, s32[]{:T(128)S(6)} %select_n.29, bf16[512,1024]{1,0:T(8,128)(2,1)} %get-tuple-element.210, pred[256]{0:T(512)(128)(4,1)S(1)} %compare_and_fusion.2), kind=kOutput, calls=%fused_computation.clone.1 | convolution fusion | flops 1890320384 | bytes 31721216 | tf_op jit(solution)/shard_map/while/body/eval_jaxpr/dot_general | solution.py:42
  347.5 15.5 %multiply_add_fusion = f32[3584,1024]{1,0:T(8,128)} fusion(f32[3584,1024]{1,0:T(8,128)} %get-tuple-element.114, f32[3584,1024]{1,0:T(8,128)} %param.12), kind=kLoop, calls=%fused_computation.9 | loop fusion | flops 11010048 | bytes 44040192 | tf_op jit(solution)/shard_map/add | solution.py:51
  (2 shorter events, 0.0 us)
Async XLA Ops:
  6.5 34.3 %all-gather.9.cloned.1.call-start = ((), (), s32[]{:S(2)}) async-start(), calls=%async_computation.5 | async-start | bytes 2359296 | tf_op jit(solution)/shard_map/all_gather | solution.py:22
  7.3 83.2 %all-gather.5.cloned.1.call-start = ((), (), s32[]{:S(2)}) async-start(), calls=%async_computation.2 | async-start | bytes 4587520 | tf_op jit(solution)/shard_map/all_gather | solution.py:10
  8.0 120.7 %reduce-scatter.5.cloned.1.call-start = ((), (), s32[]{:S(2)}) async-start(), calls=%async_computation.6 | async-start | bytes 2621440 | tf_op jit(solution)/shard_map/reduce_scatter | solution.py:23
  47.3 165.5 %copy-start = (s32[4]{0:T(128)S(1)}, s32[4]{0:T(128)}, u32[]{:S(2)}) copy-start(s32[4]{0:T(128)} %param.13) | copy-start | bytes 52
  47.3 163.4 %reduce-scatter.3.cloned.1.call-start = ((), (), s32[]{:S(2)}) async-start(), calls=%async_computation.3 | async-start | bytes 8257536 | tf_op jit(solution)/shard_map/reduce_scatter | solution.py:12
  112.1 125.5 %all-gather.11.cloned.1.call-start = ((), (), s32[]{:S(2)}) async-start(), calls=%async_computation.7 | async-start | bytes 1310720 | tf_op jit(solution)/shard_map/all_gather | solution.py:29
  130.5 151.3 %all-gather.7.cloned.1.call-start = ((), (), s32[]{:S(2)}) async-start(), calls=%async_computation.4 | async-start | bytes 4128768 | tf_op jit(solution)/shard_map/all_gather | solution.py:20
Sparse Core Ops, SparseCore 0:
  9.0 31.7 all-gather.8
  42.6 47.8 all-gather.4
  93.5 35.1 reduce-scatter.4
  131.0 79.6 reduce-scatter.2
  212.6 24.9 all-gather.10
  239.1 42.5 all-gather.6
where the time goes:
time: 370 us
  waiting for transfers between devices  243 us (66%)
  matrix products  79.4 us (21%)
  other arithmetic  21.7 us (6%)
  between operations  13.5 us (4%)
  loops' own time  7.2 us (2%)
  local copies, waits for them, and re-layouts  4.88 us (1%)
    reduce_scatter x1, waiting for transfers between devices, body(): lax.psum_scatter(lax.dot_general(basis_out, gathered, (((0,), (1,)), ((),...  80 us
    dot_general x4, matrix products, add_example(): lax.dot_general(grad_block, act_block, (((token_dim,), (0,)), ((), ())),...  51.4 us
    all_gather x1, waiting for transfers between devices, body(): lax.all_gather(scattered.astype(jnp.bfloat16), 'inp', axis=0, tiled=True)  44.2 us
    all_gather x1, waiting for transfers between devices, body(): gathered = lax.all_gather(grads, 'out', axis=0, tiled=True)  43.1 us
    all_gather x1, waiting for transfers between devices, body(): gathered_acts = lax.all_gather(acts, 'inp', axis=0, tiled=True)  32.7 us
    all_gather x1, waiting for transfers between devices, body(): lax.all_gather(act_scattered.astype(jnp.bfloat16), 'out', axis=0, tiled=T...  24.6 us
    dot_general x1, matrix products, body(): lax.dot_general(basis_out, gathered, (((0,), (1,)), ((), ())), preferred_...  21.5 us
    reduce_scatter x1, waiting for transfers between devices, body(): lax.psum_scatter(jnp.dot(gathered_acts, basis_in, preferred_element_type=...  16.6 us
  transfers between devices with their start and end apart: 6, of which 6 were waited for; matrix products, arithmetic and copies ran while one was open for 9% of the time, Pallas kernels for 0%

commit v1 on v0

v1 whole, which is shorter than its diff:
```python
import functools

import jax
import jax.numpy as jnp
from jax import lax
from jax.experimental import pallas as pl
from jax.experimental.pallas import tpu as pltpu
from jax.sharding import PartitionSpec as P

CAP = 256
GRADS_MAX, ACTS_MAX = 1.1953125, 6.0
BASIS_OUT_MAX, BASIS_IN_MAX = 0.03125, 0.0625
MESH = pl.DeviceIdType.MESH
LAG = 2
TILE = 256
HALF = TILE // 2
WIRE = jnp.int16
LEVELS = 32767.0


def encode(value, bound):
    level = jnp.sqrt(jnp.sqrt(jnp.abs(value) * (1.0 / bound))) * LEVELS + 0.5
    level = jnp.minimum(level, LEVELS).astype(jnp.int32)
    return jnp.where(value < 0, -level, level).astype(WIRE)


def decode(level, bound):
    root = level.astype(jnp.int32).astype(jnp.float32) * (1.0 / LEVELS)
    return (root * root) * (root * jnp.abs(root)) * bound


def rotate_kernel(
    nz,
    g_bound,
    a_bound,
    grads,
    acts,
    basis_out,
    basis_in,
    res,
    act_res,
    gall,
    bout,
    bin_,
    own,
    psend,
    precv,
    rsend,
    rrecv,
    aall,
    apart,
    asend,
    arecv1,
    arecv2,
    load_sem,
    basis_sem,
    g_sem,
    p_sem,
    r_sem,
    f_sem,
    q_sem,
    az_sem,
    ap_sem,
    ax_sem,
):
    o, i = lax.axis_index("out"), lax.axis_index("inp")
    z, core = i // 2, i % 2
    x, y = o % 2, o // 2
    xo, yo = y * 2 + (1 - x), (1 - y) * 2 + x
    do = (1 - y) * 2 + (1 - x)
    rows = grads.shape[0]
    tiles = basis_out.shape[1] // TILE
    per = tiles // 2
    count = 4 * per
    arows = acts.shape[0]
    right, left = (i + 2) % (2 * nz), (i + 2 * nz - 2) % (2 * nz)
    pair = z * 2 + (1 - core)
    last = nz - 1

    def remote(src, dst, sems, device):
        return pltpu.make_async_remote_copy(
            src_ref=src, dst_ref=dst, send_sem=sems[0], recv_sem=sems[1], device_id=device, device_id_type=MESH
        )

    def basis_copy(n):
        j, mine = n // 2, n % 2
        tile = jnp.where(mine == 1, core, 1 - core) * per + j
        return pltpu.make_async_copy(
            basis_out.at[:, pl.ds(pl.multiple_of(tile * TILE, TILE), TILE)], bout.at[n], basis_sem.at[n]
        )

    own_grads = pltpu.make_async_copy(grads, gall.at[o], load_sem.at[0])
    own_acts = pltpu.make_async_copy(acts, aall.at[i], load_sem.at[1])
    in_basis = pltpu.make_async_copy(basis_in, bin_, load_sem.at[2])
    own_grads.start()
    own_acts.start()
    lax.fori_loop(0, tiles, lambda n, c: (basis_copy(n).start(), c)[1], 0)
    in_basis.start()

    barrier = pltpu.get_barrier_semaphore()
    for device in ((xo, i), (yo, i), (o, pair)):
        pl.semaphore_signal(barrier, inc=1, device_id=device, device_id_type=MESH)

    @pl.when(z > 0)
    def _():
        pl.semaphore_signal(barrier, inc=1, device_id=(o, left), device_id_type=MESH)

    @pl.when(z < last)
    def _():
        pl.semaphore_signal(barrier, inc=1, device_id=(o, right), device_id_type=MESH)

    pl.semaphore_wait(barrier, 3 + (z + nz - 1) // nz + 1 - (z + 1) // nz)

    half = rows // 2

    def g_copy(which, source, lo, size, device):
        part = gall.at[source, pl.ds(lo, size), :]
        src = grads if which < 2 else part
        return remote(src, part, (g_sem.at[which, 0], g_sem.at[which, 1]), device)

    g_x, g_y = g_copy(0, o, 0, rows, (xo, i)), g_copy(1, o, 0, rows, (yo, i))
    g_x_in, g_y_in = g_copy(0, xo, 0, rows, (xo, i)), g_copy(1, yo, 0, rows, (yo, i))
    g_xy, g_yx = g_copy(2, xo, 0, half, (yo, i)), g_copy(3, yo, half, half, (xo, i))
    g_xy_in, g_yx_in = g_copy(2, do, 0, half, (yo, i)), g_copy(3, do, half, half, (xo, i))
    g_x.start()
    g_y.start()

    def az_copy(direction, hop, chip):
        block = aall.at[chip * 2 + core]
        return remote(
            acts if hop == 0 else block,
            block,
            (az_sem.at[direction, hop, 0], az_sem.at[direction, hop, 1]),
            (o, right if direction == 0 else left),
        )

    def ap_copy(chip, at_home):
        block = aall.at[chip * 2 + (core if at_home else 1 - core)]
        return remote(block, block, (ap_sem.at[chip, 0], ap_sem.at[chip, 1]), (o, pair))

    @pl.when(z < last)
    def _():
        az_copy(0, 0, z).start()

    @pl.when(z > 0)
    def _():
        az_copy(1, 0, z).start()

    own_acts.wait()
    ap_copy(z, True).start()
    own_grads.wait()

    def acts_hop(hop):
        @pl.when(z >= hop)
        def _():
            az_copy(0, hop - 1, z - hop).wait_recv()
            if hop < last:
                @pl.when(z < last)
                def _():
                    az_copy(0, hop, z - hop).start()

            ap_copy(z - hop, True).start()

        @pl.when(z + hop <= last)
        def _():
            az_copy(1, hop - 1, z + hop).wait_recv()
            if hop < last:
                @pl.when(z > 0)
                def _():
                    az_copy(1, hop, z + hop).start()

            ap_copy(z + hop, True).start()

    wide = act_res.shape[2] // 2
    first, second = (xo, yo), (yo, xo)

    def quarter(side, keep, n):
        a = x if side == 0 else y
        a = a if keep else 1 - a
        return n * 2 + a if side == 0 else a * 2 + n

    def ax(side, n):
        return ax_sem.at[side, n, 0], ax_sem.at[side, n, 1]

    def ax_first(side, n):
        return remote(
            asend.at[side, quarter(side, False, n)], arecv1.at[side, n], ax(side, n), (first[side], i)
        )

    def ax_second(side):
        q = second[side]
        return remote(asend.at[side, q], arecv2.at[side], ax(side, 2), (q, i))

    def ax_columns(q, side):
        return act_res.at[q, :, pl.ds(side * wide, wide)]

    def ax_back(side, q):
        return remote(ax_columns(q, side), ax_columns(q, side), ax(side, 3), (second[side], i))

    def ax_all(side, n, keep):
        q = quarter(side, keep, n)
        return remote(ax_columns(q, side), ax_columns(q, side), ax(side, 4 + n), (first[side], i))

    def act_product():
        in_basis.wait()
        for chip in range(nz):
            ap_copy(chip, False).wait_recv()
        blocks = aall.shape[0] // 4

        def one(q, carry):
            lhs = aall[pl.ds(q * blocks, blocks)].reshape(blocks * arows, -1)
            for side in range(2):
                value = jnp.dot(
                    lhs, bin_[:, side * wide : (side + 1) * wide], preferred_element_type=jnp.float32
                )
                apart[side, q] = value
                asend[side, q] = encode(value, a_bound)
            return carry

        lax.fori_loop(0, 4, one, 0)
        for side in range(2):
            for n in range(2):
                ax_first(side, n).start()

    def act_second():
        for side in range(2):
            for n in range(2):
                ax_first(side, n).wait_recv()
                q = quarter(side, True, n)
                apart[side, q] = apart[side, q] + decode(arecv1[side, n], a_bound)
            q = second[side]
            asend[side, q] = encode(apart[side, q], a_bound)
            ax_second(side).start()

    def act_third():
        for side in range(2):
            ax_second(side).wait_recv()
            total = apart[side, o] + decode(arecv2[side], a_bound)
            act_res[o, :, side * wide : (side + 1) * wide] = total.astype(jnp.bfloat16)
            ax_back(side, o).start()

    def act_fourth():
        for side in range(2):
            ax_back(side, second[side]).wait_recv()
            for n in range(2):
                ax_all(side, n, True).start()

    def block_of(k):
        b = k // per
        bx, by = b % 2, b // 2
        return (y + by) % 2 * 2 + (x + bx) % 2

    def pair_copy(k):
        return remote(psend.at[k], precv.at[k], (p_sem.at[k, 0], p_sem.at[k, 1]), (o, pair))

    def sum_copy(d, k):
        return remote(
            rsend.at[d, k], rrecv.at[d, k], (r_sem.at[d, k, 0], r_sem.at[d, k, 1]), (o, right if d == 0 else left)
        )

    def place(d, k, of_core):
        return res.at[of_core * per + k % per, block_of(k), :, pl.ds(d * HALF, HALF)]

    def out_copy(d, k):
        ref = place(d, k, core)
        return remote(ref, ref, (f_sem.at[d, k, 0], f_sem.at[d, k, 1]), (o, left if d == 0 else right))

    def share_copy(d, k, of_core):
        ref = place(d, k, of_core)
        return remote(ref, ref, (q_sem.at[d, k, 0], q_sem.at[d, k, 1]), (o, pair))

    def valid(k):
        return (k >= 0) & (k < count)

    def step(t, carry):
        for hop in range(1, nz):
            pl.when(t == 2 * hop)(functools.partial(acts_hop, hop))

        @pl.when(t == per)
        def _():
            g_x_in.wait_recv()
            g_xy.start()
            g_y_in.wait_recv()
            g_yx.start()

        pl.when(t == per + 2)(act_product)

        @pl.when(t == 3 * per)
        def _():
            g_xy_in.wait_recv()
            g_yx_in.wait_recv()

        pl.when(t == 3 * per - 3)(act_second)
        pl.when(t == 3 * per + 3)(act_third)
        pl.when(t == 4 * per)(act_fourth)

        @pl.when(t < count)
        def _():
            j = t % per

            @pl.when(t < per)
            def _():
                basis_copy(2 * j).wait()
                basis_copy(2 * j + 1).wait()

            lhs = gall[block_of(t)]
            psend[t] = encode(jnp.dot(lhs, bout[2 * j], preferred_element_type=jnp.float32), g_bound)
            pair_copy(t).start()
            own[t] = jnp.dot(lhs, bout[2 * j + 1], preferred_element_type=jnp.float32)

        k = t - 1

        @pl.when(valid(k))
        def _():
            pair_copy(k).wait_recv()
            own[k] = own[k] + decode(precv[k], g_bound)

        for d in range(2):
            hops = z if d == 0 else last - z
            k = t - 1 - LAG * hops

            @pl.when(valid(k))
            def _(d=d, hops=hops, k=k):
                cols = slice(d * HALF, (d + 1) * HALF)

                @pl.when(hops > 0)
                def _():
                    sum_copy(d, k).wait_recv()
                    own[k, :, cols] = own[k, :, cols] + decode(rrecv[d, k], g_bound)

                @pl.when(hops < last)
                def _():
                    rsend[d, k] = encode(own[k, :, cols], g_bound)
                    sum_copy(d, k).start()

                @pl.when(hops == last)
                def _():
                    res[core * per + k % per, block_of(k), :, cols] = own[k, :, cols].astype(jnp.bfloat16)
                    out_copy(d, k).start()
                    share_copy(d, k, core).start()

            k2 = t - 1 - LAG * last - LAG * (last - hops)

            @pl.when(valid(k2) & (hops < last))
            def _(d=d, hops=hops, k=k2):
                out_copy(d, k).wait_recv()

                @pl.when(hops > 0)
                def _():
                    out_copy(d, k).start()

                share_copy(d, k, core).start()

        return carry

    lax.fori_loop(0, count + 1 + 2 * LAG * last, step, 0)

    for side in range(2):
        for n in range(2):
            ax_all(side, n, False).wait_recv()
            ax_all(side, n, True).wait_send()
            ax_first(side, n).wait_send()
        ax_second(side).wait_send()
        ax_back(side, o).wait_send()
    for copy in (g_x, g_y, g_xy, g_yx):
        copy.wait_send()
    for chip in range(nz):
        ap_copy(chip, True).wait_send()
    for hop in range(last):
        @pl.when((z < last) & (z >= hop))
        def _(hop=hop):
            az_copy(0, hop, z - hop).wait_send()

        @pl.when((z > 0) & (z + hop <= last))
        def _(hop=hop):
            az_copy(1, hop, z + hop).wait_send()

    def finish(k, carry):
        pair_copy(k).wait_send()
        for d in range(2):
            hops = z if d == 0 else last - z
            share_copy(d, k, 1 - core).wait_recv()
            share_copy(d, k, core).wait_send()

            @pl.when(hops < last)
            def _(d=d):
                sum_copy(d, k).wait_send()

            @pl.when(hops > 0)
            def _(d=d):
                out_copy(d, k).wait_send()

        return carry

    lax.fori_loop(0, count, finish, 0)


def rotate(nz, grads, acts, basis_out, basis_in):
    rows, arows = grads.shape[0], acts.shape[0]
    depth, columns = basis_out.shape
    adepth, acolumns = basis_in.shape
    tiles = columns // TILE
    count = 4 * (tiles // 2)
    wide = acolumns // 2
    blocks = 2 * nz
    g_bound = GRADS_MAX * BASIS_OUT_MAX * depth * blocks * 1.02
    a_bound = ACTS_MAX * BASIS_IN_MAX * adepth * 4 * 1.02
    dma = pltpu.SemaphoreType.DMA
    any_spec = pl.BlockSpec(memory_space=pl.ANY)
    vmem_spec = pl.BlockSpec(memory_space=pltpu.VMEM)
    return pl.pallas_call(
        functools.partial(rotate_kernel, nz, g_bound, a_bound),
        out_shape=(
            jax.ShapeDtypeStruct((tiles, 4, rows, TILE), jnp.bfloat16),
            jax.ShapeDtypeStruct((4, blocks * arows // 4, acolumns), jnp.bfloat16),
        ),
        in_specs=[any_spec] * 4,
        out_specs=(vmem_spec, vmem_spec),
        scratch_shapes=[
            pltpu.VMEM((4, rows, depth), jnp.bfloat16),
            pltpu.VMEM((tiles, depth, TILE), jnp.bfloat16),
            pltpu.VMEM((adepth, acolumns), jnp.bfloat16),
            pltpu.VMEM((count, rows, TILE), jnp.float32),
            pltpu.VMEM((count, rows, TILE), WIRE),
            pltpu.VMEM((count, rows, TILE), WIRE),
            pltpu.VMEM((2, count, rows, HALF), WIRE),
            pltpu.VMEM((2, count, rows, HALF), WIRE),
            pltpu.VMEM((blocks, arows, adepth), jnp.bfloat16),
            pltpu.VMEM((2, 4, rows, wide), jnp.float32),
            pltpu.VMEM((2, 4, rows, wide), WIRE),
            pltpu.VMEM((2, 2, rows, wide), WIRE),
            pltpu.VMEM((2, rows, wide), WIRE),
            dma((3,)),
            dma((tiles,)),
            dma((4, 2)),
            dma((count, 2)),
            dma((2, count, 2)),
            dma((2, count, 2)),
            dma((2, count, 2)),
            dma((2, nz - 1, 2)),
            dma((nz, 2)),
            dma((2, 6, 2)),
        ],
        compiler_params=pltpu.CompilerParams(
            collective_id=0, has_side_effects=True, vmem_limit_bytes=62 * 1024 * 1024
        ),
        name="rotate",
    )(grads, acts, basis_out, basis_in)


def correct_kernel(examples, lengths, grad, act, old, out, turned, running):
    windows = grad.shape[0] // CAP
    for w in range(windows):
        turned[w] = grad[w * CAP : (w + 1) * CAP, :].T
    running[...] = jnp.zeros_like(running)
    rows = lax.broadcasted_iota(jnp.int32, (CAP, 1), 0)

    def add_example(e, offset):
        end = offset + lengths[e]
        w = jnp.minimum(offset // CAP, windows - 1)

        def part(at):
            places = at * CAP + rows
            inside = (places >= offset) & (places < end)
            block = act[pl.ds(pl.multiple_of(at * CAP, CAP), CAP), :]
            block = jnp.where(inside, block, jnp.zeros_like(block))
            return jnp.dot(turned[at], block, preferred_element_type=jnp.float32)

        @pl.when(end <= (w + 1) * CAP)
        def _():
            projected = part(w)
            running[...] += projected * projected

        @pl.when(end > (w + 1) * CAP)
        def _():
            projected = part(w) + part(w + 1)
            running[...] += projected * projected

        return end

    lax.fori_loop(0, examples, add_example, jnp.int32(0))
    out[...] = 0.8 * old[...] + 0.2 * running[...] / examples


def correct(grad, act, old, lengths):
    tiles, tokens, width = grad.shape
    columns = act.shape[1]
    examples = lengths.shape[0]
    return pl.pallas_call(
        functools.partial(correct_kernel, examples),
        out_shape=jax.ShapeDtypeStruct(old.shape, jnp.float32),
        grid_spec=pltpu.PrefetchScalarGridSpec(
            num_scalar_prefetch=1,
            grid=(tiles,),
            in_specs=[
                pl.BlockSpec((None, tokens, width), lambda n, _: (n, 0, 0)),
                pl.BlockSpec((tokens, columns), lambda n, _: (0, 0)),
                pl.BlockSpec((width, columns), lambda n, _: (n, 0)),
            ],
            out_specs=pl.BlockSpec((width, columns), lambda n, _: (n, 0)),
            scratch_shapes=[
                pltpu.VMEM((tokens // CAP, width, CAP), jnp.bfloat16),
                pltpu.VMEM((width, columns), jnp.float32),
            ],
        ),
        compiler_params=pltpu.CompilerParams(vmem_limit_bytes=40 * 1024 * 1024),
        name="correct",
    )(lengths, grad, act, old)


def gather_rotations(grads, acts, basis_out, basis_in):
    gathered = lax.all_gather(grads, "out", axis=0, tiled=True)
    scattered = lax.psum_scatter(
        jnp.dot(gathered, basis_out, preferred_element_type=jnp.float32), "inp", scatter_dimension=0, tiled=True
    )
    grad_rot = lax.all_gather(scattered.astype(jnp.bfloat16), "inp", axis=0, tiled=True)
    gathered_acts = lax.all_gather(acts, "inp", axis=0, tiled=True)
    act_scattered = lax.psum_scatter(
        jnp.dot(gathered_acts, basis_in, preferred_element_type=jnp.float32), "out", scatter_dimension=0, tiled=True
    )
    act_rot = lax.all_gather(act_scattered.astype(jnp.bfloat16), "out", axis=0, tiled=True)
    tokens, columns = grad_rot.shape
    width = min(columns, TILE) if columns % TILE == 0 else HALF
    return grad_rot.reshape(tokens, columns // width, width).transpose(1, 0, 2), act_rot


def body(outs, nz, grads, acts, basis_out, basis_in, old_correction, lengths):
    if outs == 4:
        grad, act = rotate(nz, grads, acts, basis_out, basis_in)
        tiles, blocks, rows, width = grad.shape
        grad = grad.reshape(tiles, blocks * rows, width)
        act = act.reshape(-1, act.shape[-1])
    else:
        grad, act = gather_rotations(grads, acts, basis_out, basis_in)
    return correct(grad, act, old_correction, lengths)


def solution(mesh):
    in_specs = (
        P("out", "inp"),
        P("inp", "out"),
        P("inp", "out"),
        P("out", "inp"),
        P("out", "inp"),
        P(),
    )
    run = functools.partial(body, mesh.shape["out"], mesh.shape["inp"] // 2)
    return jax.shard_map(run, mesh=mesh, in_specs=in_specs, out_specs=P("out", "inp"), check_vma=False)
```

time: 370 us -> 129 us (0.35)
  waiting for transfers between devices: 243 us -> 0 us
  Pallas kernels: 0 us -> 126 us
  matrix products: 79.4 us -> 0 us
  other arithmetic: 21.7 us -> 0 us
  between operations: 13.5 us -> 0.03 us
  loops' own time: 7.2 us -> 0 us
    all_gather x4 -> x0, waiting for transfers between devices: 145 us -> none  [the longest x1 44.2 us: body(): lax.all_gather(scattered.astype(jnp.bfloat16), 'inp', axis=0, tiled=True)]
    pallas_call x0 -> x2, Pallas kernels: none -> 126 us  [the longest x1 97.9 us: rotate(): pl.pallas_call(functools.partial(rotate_kernel, nz, g_bound, a_bound), ou...]
    reduce_scatter x2 -> x0, waiting for transfers between devices: 96.6 us -> none  [the longest x1 80 us: body(): lax.psum_scatter(lax.dot_general(basis_out, gathered, (((0,), (1,)), ((),...]
    dot_general x6 -> x0, matrix products: 79.4 us -> none  [the longest x4 51.4 us: add_example(): lax.dot_general(grad_block, act_block, (((token_dim,), (0,)), ((), ())),...]
    add x1 -> x0, other arithmetic: 15.5 us -> none  [body(): return 0.8 * old_correction + 0.2 * running / examples]
    another operation x1 -> x0, loops' own time: 7.2 us -> none  [body(): lax.fori_loop(0, examples, add_example, jnp.zeros(old_correction.shape, j...]
    dynamic_slice x8 -> x0, local copies, waits for them, and re-layouts: 4.88 us -> none  [the longest x4 2.68 us: add_example(): length = lengths[example]]
    convert_element_type x2 -> x0, other arithmetic: 3.78 us -> none  [the longest x1 2 us: body(): scattered.astype(jnp.bfloat16)]
  transfers between devices with their start and end apart: 6 -> 0, of which waited for: 6 -> 0; matrix products, arithmetic and copies ran while one was open for 9% -> 0% of each run, Pallas kernels for 0% -> 0%
where the time goes in v1:
time: 129 us; the launch traced here: 130 us
  Pallas kernels  126 us (98%)
  local copies, waits for them, and re-layouts  3.26 us (3%)
    pallas_call x1, Pallas kernels, rotate(): pl.pallas_call(functools.partial(rotate_kernel, nz, g_bound, a_bound), ou...  97.9 us
    pallas_call x1, Pallas kernels, correct(): pl.pallas_call(functools.partial(correct_kernel, examples), out_shape=jax...  28.4 us
    unnamed x6, local copies, waits for them, and re-layouts  3.26 us

profile of v1, /device:TPU:0, one launch (start us, length us, event | category | flops | bytes accessed | tf_op | source)
XLA Modules:
  0.0 129.6 jit_solution(8997068202994520311)
XLA Ops:
  0.0 0.0 copy-start.2
  0.0 97.9 %rotate.1 = (bf16[14,4,128,256]{3,2,1,0:T(8,128)(2,1)}, bf16[4,128,1024]{2,1,0:T(8,128)(2,1)}) custom-call(bf16[128,3584]{1,0:T(8,128)(2,1)} %grads.1, bf16[64,2048]{1,0:T(8,128)(2,1)} %acts.1, bf16[3584,3584]{1,0:T(8,128)(2,1)} %basis_out.1, bf16[2048,1024]{1,0:T(8,128)(2,1)} %basis_in.1), custom_call_target="tpu_custom_call" | custom-call | tf_op jit(solution)/shard_map/rotate/pallas_call | solution.py:411
  97.9 0.0 copy-done.2
  97.9 0.0 copy-start
  97.9 2.0 %copy-done = bf16[14,4,128,256]{3,2,1,0:T(8,128)(2,1)S(1)} copy-done((bf16[14,4,128,256]{3,2,1,0:T(8,128)(2,1)S(1)}, bf16[14,4,128,256]{3,2,1,0:T(8,128)(2,1)}, u32[]{:S(2)}) %copy-start) | copy-done | bytes 3670040
  99.9 0.0 copy-start.1
  99.9 1.2 copy-done.1
  101.1 28.4 %correct.1 = f32[3584,1024]{1,0:T(8,128)} custom-call(s32[4]{0:T(128)S(1)} %copy-done.2, bf16[14,512,256]{2,1,0:T(8,128)(2,1)S(1)} %bitcast.2, bf16[512,1024]{1,0:T(8,128)(2,1)S(1)} %bitcast.3, f32[3584,1024]{1,0:T(8,128)} %old.1), custom_call_target="tpu_custom_call" | custom-call | tf_op jit(solution)/shard_map/correct/pallas_call | solution.py:489
Async XLA Ops:
  0.0 97.9 %copy-start.2 = (s32[4]{0:T(128)S(1)}, s32[4]{0:T(128)}, u32[]{:S(2)}) copy-start(s32[4]{0:T(128)} %lengths.1) | copy-start | bytes 52
  97.9 2.0 %copy-start = (bf16[14,4,128,256]{3,2,1,0:T(8,128)(2,1)S(1)}, bf16[14,4,128,256]{3,2,1,0:T(8,128)(2,1)}, u32[]{:S(2)}) copy-start(bf16[14,4,128,256]{3,2,1,0:T(8,128)(2,1)} %get-tuple-element.7) | copy-start | bytes 11010052
  99.9 1.2 copy-start.1

commit v2 on v1

--- a/solution.py
+++ b/solution.py
@@ -12,6 +12,7 @@
 BASIS_OUT_MAX, BASIS_IN_MAX = 0.03125, 0.0625
 MESH = pl.DeviceIdType.MESH
 LAG = 2
+GAP = 7
 TILE = 256
 HALF = TILE // 2
 WIRE = jnp.int16
@@ -59,6 +60,7 @@
     r_sem,
     f_sem,
     q_sem,
+    s_sem,
     az_sem,
     ap_sem,
     ax_sem,
@@ -89,7 +91,7 @@
             basis_out.at[:, pl.ds(pl.multiple_of(tile * TILE, TILE), TILE)], bout.at[n], basis_sem.at[n]
         )
 
-    own_grads = pltpu.make_async_copy(grads, gall.at[o], load_sem.at[0])
+    own_grads = pltpu.make_async_copy(grads, gall.at[0], load_sem.at[0])
     own_acts = pltpu.make_async_copy(acts, aall.at[i], load_sem.at[1])
     in_basis = pltpu.make_async_copy(basis_in, bin_, load_sem.at[2])
     own_grads.start()
@@ -113,15 +115,13 @@
 
     half = rows // 2
 
-    def g_copy(which, source, lo, size, device):
-        part = gall.at[source, pl.ds(lo, size), :]
-        src = grads if which < 2 else part
+    def g_copy(which, src, slot, lo, size, device):
+        part = gall.at[slot, pl.ds(lo, size), :]
         return remote(src, part, (g_sem.at[which, 0], g_sem.at[which, 1]), device)
 
-    g_x, g_y = g_copy(0, o, 0, rows, (xo, i)), g_copy(1, o, 0, rows, (yo, i))
-    g_x_in, g_y_in = g_copy(0, xo, 0, rows, (xo, i)), g_copy(1, yo, 0, rows, (yo, i))
-    g_xy, g_yx = g_copy(2, xo, 0, half, (yo, i)), g_copy(3, yo, half, half, (xo, i))
-    g_xy_in, g_yx_in = g_copy(2, do, 0, half, (yo, i)), g_copy(3, do, half, half, (xo, i))
+    g_x, g_y = g_copy(0, grads, 1, 0, rows, (xo, i)), g_copy(1, grads, 2, 0, rows, (yo, i))
+    g_xy = g_copy(2, gall.at[1, pl.ds(0, half), :], 3, 0, half, (yo, i))
+    g_yx = g_copy(3, gall.at[2, pl.ds(half, half), :], 3, half, half, (xo, i))
     g_x.start()
     g_y.start()
 
@@ -245,115 +245,139 @@
             for n in range(2):
                 ax_all(side, n, True).start()
 
+    def slot_of(k):
+        return jnp.where(k < per, 0, jnp.where(k < 3 * per, 1 + (k - per) % 2, 3))
+
+    def tile_of(k):
+        return jnp.where(k < per, k, jnp.where(k < 3 * per, (k - per) // 2, k - 3 * per))
+
     def block_of(k):
-        b = k // per
-        bx, by = b % 2, b // 2
-        return (y + by) % 2 * 2 + (x + bx) % 2
+        slot = slot_of(k)
+        return (y + slot // 2) % 2 * 2 + (x + slot % 2) % 2
 
     def pair_copy(k):
-        return remote(psend.at[k], precv.at[k], (p_sem.at[k, 0], p_sem.at[k, 1]), (o, pair))
+        return remote(psend.at[k], precv.at[k], (s_sem.at[0], p_sem.at[k]), (o, pair))
 
     def sum_copy(d, k):
-        return remote(
-            rsend.at[d, k], rrecv.at[d, k], (r_sem.at[d, k, 0], r_sem.at[d, k, 1]), (o, right if d == 0 else left)
-        )
-
-    def place(d, k, of_core):
-        return res.at[of_core * per + k % per, block_of(k), :, pl.ds(d * HALF, HALF)]
+        return remote(rsend.at[d, k], rrecv.at[d, k], (s_sem.at[1 + d], r_sem.at[d, k]), (o, right if d == 0 else left))
+
+    def place(d, k):
+        return res.at[
+            core * per + tile_of(k), pl.ds(d * HALF, HALF), pl.ds(pl.multiple_of(block_of(k) * rows, rows), rows)
+        ]
 
     def out_copy(d, k):
-        ref = place(d, k, core)
-        return remote(ref, ref, (f_sem.at[d, k, 0], f_sem.at[d, k, 1]), (o, left if d == 0 else right))
-
-    def share_copy(d, k, of_core):
-        ref = place(d, k, of_core)
-        return remote(ref, ref, (q_sem.at[d, k, 0], q_sem.at[d, k, 1]), (o, pair))
-
-    def valid(k):
-        return (k >= 0) & (k < count)
+        ref = place(d, k)
+        return remote(ref, ref, (s_sem.at[3 + d], f_sem.at[d, k]), (o, left if d == 0 else right))
+
+    def share_copy(d, k):
+        ref = place(d, k)
+        return remote(ref, ref, (s_sem.at[5], q_sem.at[0]), (o, pair))
+
+    def chunk(v):
+        return jnp.where(v < per, v, v - GAP)
+
+    def valid(v):
+        return ((v >= 0) & (v < per)) | ((v >= per + GAP) & (v < count + GAP))
+
+    def product(lhs, k, j, blocks):
+        theirs = jnp.dot(lhs, bout[2 * j], preferred_element_type=jnp.float32)
+        for n in range(blocks):
+            psend[k + n] = encode(theirs[n * rows : (n + 1) * rows], g_bound)
+            pair_copy(k + n).start()
+        mine = jnp.dot(lhs, bout[2 * j + 1], preferred_element_type=jnp.float32)
+        for n in range(blocks):
+            own[k + n] = mine[n * rows : (n + 1) * rows]
 
     def step(t, carry):
         for hop in range(1, nz):
             pl.when(t == 2 * hop)(functools.partial(acts_hop, hop))
 
-        @pl.when(t == per)
-        def _():
-            g_x_in.wait_recv()
+        u = t - GAP
+
+        @pl.when(u == per)
+        def _():
+            g_x.wait_recv()
             g_xy.start()
-            g_y_in.wait_recv()
+            g_y.wait_recv()
             g_yx.start()
 
-        pl.when(t == per + 2)(act_product)
-
-        @pl.when(t == 3 * per)
-        def _():
-            g_xy_in.wait_recv()
-            g_yx_in.wait_recv()
-
-        pl.when(t == 3 * per - 3)(act_second)
-        pl.when(t == 3 * per + 3)(act_third)
-        pl.when(t == 4 * per)(act_fourth)
-
-        @pl.when(t < count)
-        def _():
-            j = t % per
-
-            @pl.when(t < per)
-            def _():
-                basis_copy(2 * j).wait()
-                basis_copy(2 * j + 1).wait()
-
-            lhs = gall[block_of(t)]
-            psend[t] = encode(jnp.dot(lhs, bout[2 * j], preferred_element_type=jnp.float32), g_bound)
-            pair_copy(t).start()
-            own[t] = jnp.dot(lhs, bout[2 * j + 1], preferred_element_type=jnp.float32)
-
-        k = t - 1
-
-        @pl.when(valid(k))
-        def _():
+        @pl.when(u == 3 * per)
+        def _():
+            g_xy.wait_recv()
+            g_yx.wait_recv()
+
+        pl.when(u == per + 8)(act_product)
+        pl.when(u == 3 * per)(act_second)
+        pl.when(u == 3 * per + 4)(act_third)
+        pl.when(u == 4 * per)(act_fourth)
+
+        @pl.when(t < per)
+        def _():
+            basis_copy(2 * t).wait()
+            basis_copy(2 * t + 1).wait()
+            product(gall[0], t, t, 1)
+
+        @pl.when((u >= per) & (u < 3 * per) & ((u - per) % 2 == 0))
+        def _():
+            product(gall[1:3].reshape(2 * rows, -1), u, (u - per) // 2, 2)
+
+        @pl.when((u >= 3 * per) & (u < count))
+        def _():
+            product(gall[3], u, u - 3 * per, 1)
+
+        v = t - 1
+
+        @pl.when(valid(v))
+        def _():
+            k = chunk(v)
             pair_copy(k).wait_recv()
             own[k] = own[k] + decode(precv[k], g_bound)
 
         for d in range(2):
             hops = z if d == 0 else last - z
-            k = t - 1 - LAG * hops
-
-            @pl.when(valid(k))
-            def _(d=d, hops=hops, k=k):
+            v = t - 1 - LAG * hops
+
+            @pl.when(valid(v))
+            def _(d=d, hops=hops, v=v):
+                k = chunk(v)
                 cols = slice(d * HALF, (d + 1) * HALF)
 
-                @pl.when(hops > 0)
-                def _():
-                    sum_copy(d, k).wait_recv()
-                    own[k, :, cols] = own[k, :, cols] + decode(rrecv[d, k], g_bound)
-
-                @pl.when(hops < last)
+                @pl.when(hops == 0)
                 def _():
                     rsend[d, k] = encode(own[k, :, cols], g_bound)
                     sum_copy(d, k).start()
 
+                @pl.when((hops > 0) & (hops < last))
+                def _():
+                    sum_copy(d, k).wait_recv()
+                    rsend[d, k] = encode(own[k, :, cols] + decode(rrecv[d, k], g_bound), g_bound)
+                    sum_copy(d, k).start()
+
                 @pl.when(hops == last)
                 def _():
-                    res[core * per + k % per, block_of(k), :, cols] = own[k, :, cols].astype(jnp.bfloat16)
+                    sum_copy(d, k).wait_recv()
+                    total = own[k, :, cols] + decode(rrecv[d, k], g_bound)
+                    place(d, k)[...] = total.T.astype(jnp.bfloat16)
                     out_copy(d, k).start()
-                    share_copy(d, k, core).start()
-
-            k2 = t - 1 - LAG * last - LAG * (last - hops)
-
-            @pl.when(valid(k2) & (hops < last))
-            def _(d=d, hops=hops, k=k2):
+                    share_copy(d, k).start()
+
+            v2 = t - 1 - LAG * last - LAG * (last - hops)
+
+            @pl.when(valid(v2) & (hops < last))
+            def _(d=d, hops=hops, v=v2):
+                k = chunk(v)
                 out_copy(d, k).wait_recv()
 
                 @pl.when(hops > 0)
                 def _():
                     out_copy(d, k).start()
 
-                share_copy(d, k, core).start()
+                share_copy(d, k).start()
 
         return carry
 
-    lax.fori_loop(0, count + 1 + 2 * LAG * last, step, 0)
+    lax.fori_loop(0, count + GAP + 1 + 2 * LAG * last, step, 0)
 
     for side in range(2):
         for n in range(2):
@@ -375,24 +399,23 @@
         def _(hop=hop):
             az_copy(1, hop, z + hop).wait_send()
 
-    def finish(k, carry):
-        pair_copy(k).wait_send()
-        for d in range(2):
-            hops = z if d == 0 else last - z
-            share_copy(d, k, 1 - core).wait_recv()
-            share_copy(d, k, core).wait_send()
-
-            @pl.when(hops < last)
-            def _(d=d):
-                sum_copy(d, k).wait_send()
-
-            @pl.when(hops > 0)
-            def _(d=d):
-                out_copy(d, k).wait_send()
-
-        return carry
-
-    lax.fori_loop(0, count, finish, 0)
+    def whole(ref, send, recv=0):
+        return remote(ref, ref, (s_sem.at[send], q_sem.at[recv]), (o, pair))
+
+    whole(psend, 0).wait_send()
+    for d in range(2):
+        hops = z if d == 0 else last - z
+
+        @pl.when(hops < last)
+        def _(d=d):
+            whole(rsend.at[d], 1 + d).wait_send()
+
+        @pl.when(hops > 0)
+        def _(d=d):
+            whole(res.at[pl.ds(core * per, per), pl.ds(d * HALF, HALF), :], 3 + d).wait_send()
+
+    whole(res.at[pl.ds(core * per, per)], 5).wait_send()
+    whole(res.at[pl.ds((1 - core) * per, per)], 5).wait_recv()
 
 
 def rotate(nz, grads, acts, basis_out, basis_in):
@@ -411,7 +434,7 @@
     return pl.pallas_call(
         functools.partial(rotate_kernel, nz, g_bound, a_bound),
         out_shape=(
-            jax.ShapeDtypeStruct((tiles, 4, rows, TILE), jnp.bfloat16),
+            jax.ShapeDtypeStruct((tiles, TILE, 4 * rows), jnp.bfloat16),
             jax.ShapeDtypeStruct((4, blocks * arows // 4, acolumns), jnp.bfloat16),
         ),
         in_specs=[any_spec] * 4,
@@ -433,10 +456,11 @@
             dma((3,)),
             dma((tiles,)),
             dma((4, 2)),
-            dma((count, 2)),
-            dma((2, count, 2)),
-            dma((2, count, 2)),
-            dma((2, count, 2)),
+            dma((count,)),
+            dma((2, count)),
+            dma((2, count)),
+            dma((1,)),
+            dma((6,)),
             dma((2, nz - 1, 2)),
             dma((nz, 2)),
             dma((2, 6, 2)),
@@ -448,62 +472,67 @@
     )(grads, acts, basis_out, basis_in)
 
 
-def correct_kernel(examples, lengths, grad, act, old, out, turned, running):
-    windows = grad.shape[0] // CAP
-    for w in range(windows):
-        turned[w] = grad[w * CAP : (w + 1) * CAP, :].T
-    running[...] = jnp.zeros_like(running)
-    rows = lax.broadcasted_iota(jnp.int32, (CAP, 1), 0)
-
-    def add_example(e, offset):
-        end = offset + lengths[e]
-        w = jnp.minimum(offset // CAP, windows - 1)
-
-        def part(at):
-            places = at * CAP + rows
-            inside = (places >= offset) & (places < end)
-            block = act[pl.ds(pl.multiple_of(at * CAP, CAP), CAP), :]
-            block = jnp.where(inside, block, jnp.zeros_like(block))
-            return jnp.dot(turned[at], block, preferred_element_type=jnp.float32)
-
-        @pl.when(end <= (w + 1) * CAP)
-        def _():
-            projected = part(w)
-            running[...] += projected * projected
-
-        @pl.when(end > (w + 1) * CAP)
-        def _():
-            projected = part(w) + part(w + 1)
-            running[...] += projected * projected
-
-        return end
-
-    lax.fori_loop(0, examples, add_example, jnp.int32(0))
-    out[...] = 0.8 * old[...] + 0.2 * running[...] / examples
+def correct_kernel(examples, lengths, grad, act, old, out, masked):
+    windows = act.shape[0] // CAP
+    columns = act.shape[1]
+    offsets = [jnp.int32(0)]
+    for e in range(examples):
+        offsets.append(offsets[e] + lengths[e])
+
+    def window(e):
+        return jnp.minimum(offsets[e] // CAP, windows - 1)
+
+    @pl.when(pl.program_id(0) == 0)
+    def _():
+        rows = lax.broadcasted_iota(jnp.int32, (CAP, 1), 0)
+        for e in range(examples):
+            for n in range(2):
+                at = jnp.minimum(window(e) + n, windows - 1)
+                places = (window(e) + n) * CAP + rows
+                block = act[pl.ds(pl.multiple_of(at * CAP, CAP), CAP), :]
+                inside = (places >= offsets[e]) & (places < offsets[e + 1])
+                masked[e, n] = jnp.where(inside, block, jnp.zeros_like(block))
+
+    scale = 0.2 / examples
+    width = min(columns, TILE)
+    for e in range(examples):
+        first = window(e)
+
+        def add(parts, e=e, first=first):
+            lhs = [grad[:, pl.ds(pl.multiple_of((first + n) * CAP, CAP), CAP)] for n in range(parts)]
+            for c in range(0, columns, width):
+                cols = slice(c, c + width)
+                projected = jnp.dot(lhs[0], masked[e, 0, :, cols], preferred_element_type=jnp.float32)
+                if parts == 2:
+                    projected += jnp.dot(lhs[1], masked[e, 1, :, cols], preferred_element_type=jnp.float32)
+                base = 0.8 * old[:, cols] if e == 0 else out[:, cols]
+                out[:, cols] = base + scale * (projected * projected)
+
+        crosses = offsets[e + 1] > (first + 1) * CAP
+        pl.when(crosses)(functools.partial(add, 2))
+        pl.when(jnp.logical_not(crosses))(functools.partial(add, 1))
 
 
 def correct(grad, act, old, lengths):
-    tiles, tokens, width = grad.shape
+    total, tokens = grad.shape
     columns = act.shape[1]
     examples = lengths.shape[0]
+    height = next(n for n in (512, 448, 256, 128) if total % n == 0)
     return pl.pallas_call(
         functools.partial(correct_kernel, examples),
         out_shape=jax.ShapeDtypeStruct(old.shape, jnp.float32),
         grid_spec=pltpu.PrefetchScalarGridSpec(
             num_scalar_prefetch=1,
-            grid=(tiles,),
+            grid=(total // height,),
             in_specs=[
-                pl.BlockSpec((None, tokens, width), lambda n, _: (n, 0, 0)),
+                pl.BlockSpec((height, tokens), lambda n, _: (n, 0)),
                 pl.BlockSpec((tokens, columns), lambda n, _: (0, 0)),
-                pl.BlockSpec((width, columns), lambda n, _: (n, 0)),
+                pl.BlockSpec((height, columns), lambda n, _: (n, 0)),
             ],
-            out_specs=pl.BlockSpec((width, columns), lambda n, _: (n, 0)),
-            scratch_shapes=[
-                pltpu.VMEM((tokens // CAP, width, CAP), jnp.bfloat16),
-                pltpu.VMEM((width, columns), jnp.float32),
-            ],
+            out_specs=pl.BlockSpec((height, columns), lambda n, _: (n, 0)),
+            scratch_shapes=[pltpu.VMEM((examples, 2, CAP, columns), jnp.bfloat16)],
         ),
-        compiler_params=pltpu.CompilerParams(vmem_limit_bytes=40 * 1024 * 1024),
+        compiler_params=pltpu.CompilerParams(vmem_limit_bytes=62 * 1024 * 1024),
         name="correct",
     )(lengths, grad, act, old)
 
@@ -511,7 +540,7 @@
 def gather_rotations(grads, acts, basis_out, basis_in):
     gathered = lax.all_gather(grads, "out", axis=0, tiled=True)
     scattered = lax.psum_scatter(
-        jnp.dot(gathered, basis_out, preferred_element_type=jnp.float32), "inp", scatter_dimension=0, tiled=True
+        lax.dot_general(basis_out, gathered, (((0,), (1,)), ((), ())), preferred_element_type=jnp.float32), "inp", scatter_dimension=0, tiled=True
     )
     grad_rot = lax.all_gather(scattered.astype(jnp.bfloat16), "inp", axis=0, tiled=True)
     gathered_acts = lax.all_gather(acts, "inp", axis=0, tiled=True)
@@ -519,16 +548,13 @@
         jnp.dot(gathered_acts, basis_in, preferred_element_type=jnp.float32), "out", scatter_dimension=0, tiled=True
     )
     act_rot = lax.all_gather(act_scattered.astype(jnp.bfloat16), "out", axis=0, tiled=True)
-    tokens, columns = grad_rot.shape
-    width = min(columns, TILE) if columns % TILE == 0 else HALF
-    return grad_rot.reshape(tokens, columns // width, width).transpose(1, 0, 2), act_rot
+    return grad_rot, act_rot
 
 
 def body(outs, nz, grads, acts, basis_out, basis_in, old_correction, lengths):
     if outs == 4:
         grad, act = rotate(nz, grads, acts, basis_out, basis_in)
-        tiles, blocks, rows, width = grad.shape
-        grad = grad.reshape(tiles, blocks * rows, width)
+        grad = grad.reshape(-1, grad.shape[-1])
         act = act.reshape(-1, act.shape[-1])
     else:
         grad, act = gather_rotations(grads, acts, basis_out, basis_in)

time: 129 us -> 123 us (0.953)
  local copies, waits for them, and re-layouts: 3.26 us -> 0 us
  Pallas kernels: 126 us -> 123 us
    pallas_call x1, Pallas kernels: 28.4 us -> 19.4 us  [correct(): pl.pallas_call(functools.partial(correct_kernel, examples), out_shape=jax...]
    pallas_call x1, Pallas kernels: 97.9 us -> 103 us  [rotate(): pl.pallas_call(functools.partial(rotate_kernel, nz, g_bound, a_bound), ou...]
    unnamed x6 -> x0, local copies, waits for them, and re-layouts: 3.26 us -> none
where the time goes in v2:
time: 123 us
  Pallas kernels  123 us (100%)
    pallas_call x1, Pallas kernels, rotate(): pl.pallas_call(functools.partial(rotate_kernel, nz, g_bound, a_bound), ou...  103 us
    pallas_call x1, Pallas kernels, correct(): pl.pallas_call(functools.partial(correct_kernel, examples), out_shape=jax...  19.4 us

profile of v2, /device:TPU:0, one launch (start us, length us, event | category | flops | bytes accessed | tf_op | source)
XLA Modules:
  0.0 122.6 jit_solution(7916135097640464634)
XLA Ops:
  0.0 103.1 %rotate.1 = (bf16[14,256,512]{2,1,0:T(8,128)(2,1)}, bf16[4,128,1024]{2,1,0:T(8,128)(2,1)}) custom-call(bf16[128,3584]{1,0:T(8,128)(2,1)} %grads.1, bf16[64,2048]{1,0:T(8,128)(2,1)} %acts.1, bf16[3584,3584]{1,0:T(8,128)(2,1)} %basis_out.1, bf16[2048,1024]{1,0:T(8,128)(2,1)} %basis_in.1), custom_call_target="tpu_custom_call" | custom-call | tf_op jit(solution)/shard_map/rotate/pallas_call | solution.py:434
  103.1 19.4 %correct.1 = f32[3584,1024]{1,0:T(8,128)} custom-call(s32[4]{0:T(128)} %lengths.1, bf16[3584,512]{1,0:T(8,128)(2,1)} %bitcast.2, bf16[512,1024]{1,0:T(8,128)(2,1)} %bitcast.3, f32[3584,1024]{1,0:T(8,128)} %old.1), custom_call_target="tpu_custom_call" | custom-call | tf_op jit(solution)/shard_map/correct/pallas_call | solution.py:521
